TPU v7x, 32 devices: a whole 2x2x4 slice. The times are simulated.
32 devices in a mesh: row: 4 (over y, x), col: 8 (over z, core).
Axes of the slice: x: 2, y: 2, z: 4, core: 2. Of those that a mesh axis runs over, the one named last changes fastest.
Arguments:
- tokens: bfloat16 [512, 8192], P('col', 'row'), may hold values from -6 to 6
- cotangent: bfloat16 [512, 8192], P('col', 'row'), may hold values from -6 to 6
- gate_weight: bfloat16 [8192, 32768], P('row', 'col'), may hold values from -0.125 to 0.125
- up_weight: bfloat16 [8192, 32768], P('row', 'col'), may hold values from -0.125 to 0.125
- down_weight: bfloat16 [32768, 8192], P('col', 'row'), may hold values from -0.0625 to 0.0625
- block_mask: int32 [3, 16, 64], P(None, 'row', 'col'), may hold values 0 or 1
Outputs:
- input_grad: bfloat16 [512, 8192], P('col', 'row')
- gate_grad: bfloat16 [8192, 32768], P('row', 'col')
- up_grad: bfloat16 [8192, 32768], P('row', 'col')
- down_grad: bfloat16 [32768, 8192], P('col', 'row')
All inputs are finite; a program needn't handle non-finite values. No bound on the sum of `block_mask` on one device may be relied on, other than what follows from the above.
Results may differ from a plain program's by a relative error of at most 0.005.
Values may be sent and summed in bfloat16 or wider, within the bound.
A program may use at most 256 MiB of HBM per device.

v0:
```python
import functools

import jax
import jax.numpy as jnp
from jax import lax
from jax.experimental import pallas as pl
from jax.experimental.pallas import tpu as pltpu
from jax.sharding import PartitionSpec as P

BLK = 512
VMEM_LIMIT = 40 * 1024 * 1024

NN = (((1,), (0,)), ((), ()))
NT = (((1,), (1,)), ((), ()))
TN = (((0,), (0,)), ((), ()))


def dot(a, b, dims):
    return lax.dot_general(a, b, dims, preferred_element_type=jnp.float32)


def forward_kernel(flags, acts, *refs, kinds):
    count = len(kinds)
    weights = refs[:count]
    keep, give, acc = refs[count:]
    inner, step = pl.program_id(0), pl.program_id(1)
    group, steps = pl.num_programs(0), pl.num_programs(1)

    @pl.when(step == 0)
    def _():
        acc[...] = jnp.zeros_like(acc)

    for i, kind in enumerate(kinds):

        @pl.when(flags[1 + (kind * steps + step) * group + inner] != 0)
        def _(i=i, kind=kind):
            acc[i] += dot(acts[...], weights[i][...], NT if kind == 2 else NN)

    @pl.when(step == steps - 1)
    def _():
        half = acc.shape[1] // 2
        mine = pl.multiple_of(flags[0] * half, half)
        other = pl.multiple_of((1 - flags[0]) * half, half)
        for i in range(count):
            keep[i] = acc[i, pl.ds(mine, half), :]
            give[i] = acc[i, pl.ds(other, half), :].astype(give.dtype)


def forward(flags, acts, weights, kinds, start, group, wire):
    tokens, width = acts.shape
    steps = width // BLK
    count = len(kinds)
    half = (count, tokens // 2, group * BLK)
    weight_specs = [
        pl.BlockSpec(
            (BLK, BLK),
            (lambda j, d, f: (start + j, d)) if kind == 2 else (lambda j, d, f: (d, start + j)),
        )
        for kind in kinds
    ]
    return pl.pallas_call(
        functools.partial(forward_kernel, kinds=kinds),
        grid_spec=pltpu.PrefetchScalarGridSpec(
            num_scalar_prefetch=1,
            grid=(group, steps),
            in_specs=[pl.BlockSpec((tokens, BLK), lambda j, d, f: (0, d))] + weight_specs,
            out_specs=[pl.BlockSpec((count, tokens // 2, BLK), lambda j, d, f: (0, 0, j))] * 2,
            scratch_shapes=[pltpu.VMEM((count, tokens, BLK), jnp.float32)],
        ),
        out_shape=[jax.ShapeDtypeStruct(half, jnp.float32), jax.ShapeDtypeStruct(half, wire)],
        compiler_params=pltpu.CompilerParams(vmem_limit_bytes=VMEM_LIMIT),
        cost_estimate=pl.CostEstimate(
            flops=2 * count * tokens * width * BLK * group,
            bytes_accessed=group * (count * (2 * width * BLK + 3 * tokens * BLK) + 2 * width * tokens),
            transcendentals=0,
        ),
        name="forward_part",
    )(flags, acts, *weights)


def input_kernel(flags, near, far, gate, up, *refs):
    acc = refs[-1]
    step, inner = pl.program_id(0), pl.program_id(1)
    steps, group = pl.num_programs(0), pl.num_programs(1)

    @pl.when(inner == 0)
    def _():
        acc[...] = refs[0][...] if len(refs) == 2 else jnp.zeros_like(acc)

    half = near.shape[1]
    for kind, weight in ((0, gate), (1, up)):

        @pl.when(flags[1 + (kind * steps + step) * group + inner] != 0)
        def _(kind=kind, weight=weight):
            for delta, place in ((near, flags[0]), (far, 1 - flags[0])):
                rows = pl.ds(pl.multiple_of(place * half, half), half)
                acc[rows, :] += dot(delta[kind], weight[...], NT)


def add_input_grad(flags, near, far, gate_weight, up_weight, total, start, group):
    half = near.shape[1]
    tokens, width = 2 * half, gate_weight.shape[0]
    delta_spec = pl.BlockSpec((2, half, BLK), lambda d, j, f: (0, 0, j))
    weight_spec = pl.BlockSpec((BLK, BLK), lambda d, j, f: (d, start + j))
    acc_spec = pl.BlockSpec((tokens, BLK), lambda d, j, f: (0, d))
    first = total is None
    return pl.pallas_call(
        input_kernel,
        grid_spec=pltpu.PrefetchScalarGridSpec(
            num_scalar_prefetch=1,
            grid=(width // BLK, group),
            in_specs=[delta_spec] * 2 + [weight_spec] * 2 + ([] if first else [acc_spec]),
            out_specs=acc_spec,
        ),
        out_shape=jax.ShapeDtypeStruct((tokens, width), jnp.float32),
        input_output_aliases={} if first else {5: 0},
        compiler_params=pltpu.CompilerParams(vmem_limit_bytes=VMEM_LIMIT),
        cost_estimate=pl.CostEstimate(
            flops=4 * tokens * width * BLK * group,
            bytes_accessed=4 * width * BLK * group + 8 * tokens * width,
            transcendentals=0,
        ),
        name="input_grad_part",
    )(flags, near, far, gate_weight, up_weight, *([] if first else [total]))


def weight_kernel(flags, near, far, tokens, cotan, *refs):
    grads = refs[-3:]
    step, inner = pl.program_id(0), pl.program_id(1)
    steps, group = pl.num_programs(0), pl.num_programs(1)
    half = near.shape[1]
    columns = pl.ds(pl.multiple_of(inner * BLK, BLK), BLK)
    mine = pl.ds(pl.multiple_of(flags[0] * half, half), half)
    other = pl.ds(pl.multiple_of((1 - flags[0]) * half, half), half)
    for kind, grad in enumerate(grads):
        kept = flags[1 + (kind * steps + step) * group + inner] != 0

        @pl.when(kept)
        def _(kind=kind, grad=grad):
            one, two = near[kind, :, columns], far[kind, :, columns]
            if kind == 2:
                value = dot(one, cotan[mine, :], TN) + dot(two, cotan[other, :], TN)
            else:
                value = dot(tokens[mine, :], one, TN) + dot(tokens[other, :], two, TN)
            grad[...] = value.astype(grad.dtype)

        @pl.when(jnp.logical_not(kept))
        def _(grad=grad):
            grad[...] = jnp.zeros_like(grad)


def weight_grads(flags, near, far, tokens_all, cotan_all, grads, hidden, start, group):
    tokens, width = tokens_all.shape
    act_spec = pl.BlockSpec((tokens, BLK), lambda d, j, f: (0, d))
    delta_spec = pl.BlockSpec(near.shape, lambda d, j, f: (0, 0, 0))
    grad_spec = pl.BlockSpec((BLK, BLK), lambda d, j, f: (d, start + j))
    down_spec = pl.BlockSpec((BLK, BLK), lambda d, j, f: (start + j, d))
    any_spec = pl.BlockSpec(memory_space=pl.ANY)
    first = grads is None
    return pl.pallas_call(
        weight_kernel,
        grid_spec=pltpu.PrefetchScalarGridSpec(
            num_scalar_prefetch=1,
            grid=(width // BLK, group),
            in_specs=[delta_spec] * 2 + [act_spec] * 2 + ([] if first else [any_spec] * 3),
            out_specs=[grad_spec, grad_spec, down_spec],
        ),
        out_shape=[
            jax.ShapeDtypeStruct((width, hidden), jnp.bfloat16),
            jax.ShapeDtypeStruct((width, hidden), jnp.bfloat16),
            jax.ShapeDtypeStruct((hidden, width), jnp.bfloat16),
        ],
        input_output_aliases={} if first else {5: 0, 6: 1, 7: 2},
        compiler_params=pltpu.CompilerParams(vmem_limit_bytes=VMEM_LIMIT),
        cost_estimate=pl.CostEstimate(
            flops=6 * tokens * width * BLK * group,
            bytes_accessed=6 * width * BLK * group + 4 * tokens * width,
            transcendentals=0,
        ),
        name="weight_grad_part",
    )(flags, near, far, tokens_all, cotan_all, *([] if first else grads))


def swiglu(gate_value, up_value, hidden_grad):
    sigmoid = jax.nn.sigmoid(gate_value)
    swish = gate_value * sigmoid
    hidden = swish * up_value
    gate_delta = hidden_grad * up_value * sigmoid * (1.0 + gate_value * (1.0 - sigmoid))
    up_delta = hidden_grad * swish
    return jnp.stack([gate_delta, up_delta, hidden]).astype(jnp.bfloat16)


def shards(tokens, cotangent, gate_weight, up_weight, down_weight, block_mask):
    rows = lax.axis_size("row")
    levels = rows.bit_length() - 1
    row = lax.axis_index("row")
    wire = jnp.bfloat16 if rows <= 4 else jnp.float32
    hidden = gate_weight.shape[1]
    blocks = hidden // BLK
    group = 2 if blocks % 2 == 0 else 1
    groups = blocks // group

    def swap(part, bit):
        return lax.ppermute(part, "row", [(i, i ^ (1 << bit)) for i in range(rows)])

    def side(bit):
        return (row >> bit) & 1

    def after(value, earlier):
        return lax.optimization_barrier((value, earlier))

    def finish_sum(value, slope, order):
        got = swap(value[1], order[0])
        give, got = after(slope[1], got)
        parts = [
            value[0] + got.astype(jnp.float32),
            slope[0] + swap(give, order[0]).astype(jnp.float32),
        ]
        for bit in order[1:]:
            half = parts[0].shape[1] // 2
            mine = [lax.dynamic_slice_in_dim(p, side(bit) * half, half, 1) for p in parts]
            other = [lax.dynamic_slice_in_dim(p, (1 - side(bit)) * half, half, 1) for p in parts]
            got = swap(jnp.concatenate([p.astype(wire) for p in other]), bit)
            parts = [
                mine[0] + got[: mine[0].shape[0]].astype(jnp.float32),
                mine[1] + got[mine[0].shape[0] :].astype(jnp.float32),
            ]
        return parts

    def spread(part, order):
        for bit in reversed(order[1:]):
            got = swap(part, bit)
            low = jnp.where(side(bit) == 0, part, got)
            high = jnp.where(side(bit) == 0, got, part)
            part = jnp.concatenate([low, high], axis=1)
        return part, swap(part, order[0])

    orders = [
        tuple(range(levels)) if g % 2 == 0 else tuple(reversed(range(levels)))
        for g in range(groups)
    ]
    flags = [
        jnp.concatenate(
            [
                side(order[0]).reshape(1).astype(jnp.int32),
                block_mask[:, :, g * group : (g + 1) * group].reshape(-1),
            ]
        )
        for g, order in enumerate(orders)
    ]

    tokens_all = lax.all_gather(tokens, "col", axis=0, tiled=True)
    cotan_all = lax.all_gather(cotangent, "col", axis=0, tiled=True)

    values, slopes, last = [], [], None
    for acts, weights, kinds, results in (
        (tokens_all, [gate_weight, up_weight], (0, 1), values),
        (cotan_all, [down_weight], (2,), slopes),
    ):
        for g in range(groups):
            order_flags = flags[g]
            if last is not None:
                order_flags, last[0] = after(order_flags, last[0])
            last = list(forward(order_flags, acts, weights, kinds, g * group, group, wire))
            results.append(last)
    total, halves = None, []
    for g in range(groups):
        pair, slope = finish_sum(values[g], slopes[g], orders[g])
        near, far = spread(swiglu(pair[0], pair[1], slope[0]), orders[g])
        halves.append((near, far))
        total = add_input_grad(
            flags[g], near, far, gate_weight, up_weight, total, g * group, group
        )
    input_grad = lax.psum_scatter(total, "col", scatter_dimension=0, tiled=True)
    grads = None
    for g, (near, far) in enumerate(halves):
        grads = weight_grads(
            flags[g], near, far, tokens_all, cotan_all, grads, hidden, g * group, group
        )
    return (input_grad.astype(jnp.bfloat16), *grads)


def solution(mesh):
    in_specs = (
        P("col", "row"),
        P("col", "row"),
        P("row", "col"),
        P("row", "col"),
        P("col", "row"),
        P(None, "row", "col"),
    )
    out_specs = (P("col", "row"), P("row", "col"), P("row", "col"), P("col", "row"))
    return jax.shard_map(shards, mesh=mesh, in_specs=in_specs, out_specs=out_specs, check_vma=False)
```

profile of v0, /device:TPU:0, one launch (start us, length us, event | category | flops | bytes accessed | tf_op | source)
XLA Modules:
  0.0 350.0 jit_solution(14215668668661016935)
XLA Ops:
  10.2 31.3 %all-gather.3.cloned.1.call-done.acts.tokens = bf16[512,2048]{1,0:T(8,128)(2,1)} async-done(((bf16[64,2048]{1,0:T(8,128)(2,1)}), bf16[512,2048]{1,0:T(8,128)(2,1)}) %all-gather.3.cloned.1.call-update) | async-done | bytes 2097168 | tf_op jit(solution)/shard_map/all_gather | solution.py:252
  43.0 9.4 %forward_part.8 = (f32[2,256,1024]{2,1,0:T(8,128)S(1)}, bf16[2,256,1024]{2,1,0:T(8,128)(2,1)}) custom-call(s32[25]{0:T(128)S(1)} %get-tuple-element.61.flags, bf16[512,2048]{1,0:T(8,128)(2,1)S(1)} %copy-done.1, bf16[2048,4096]{1,0:T(8,128)(2,1)} %gate.7, bf16[2048,4096]{1,0:T(8,128)(2,1)} %up.7), custom_call_target="tpu_custom_call" | custom-call | flops 4294967296 | bytes 15728640 | tf_op jit(solution)/shard_map/forward_part/pallas_call | solution.py:61
  53.1 9.0 %forward_part.9 = (f32[2,256,1024]{2,1,0:T(8,128)S(1)}, bf16[2,256,1024]{2,1,0:T(8,128)(2,1)}) custom-call(s32[25]{0:T(128)S(1)} %get-tuple-element.63.flags, bf16[512,2048]{1,0:T(8,128)(2,1)S(1)} %copy-done.1, bf16[2048,4096]{1,0:T(8,128)(2,1)} %gate.7, bf16[2048,4096]{1,0:T(8,128)(2,1)} %up.7), custom_call_target="tpu_custom_call" | custom-call | flops 4294967296 | bytes 15728640 | tf_op jit(solution)/shard_map/forward_part/pallas_call | solution.py:61
  62.2 4.0 %collective-permute-start.10 = (bf16[2,256,1024]{2,1,0:T(8,128)(2,1)}, bf16[2,256,1024]{2,1,0:T(8,128)(2,1)}, u32[]{:S(2)}, u32[]{:S(2)}) collective-permute-start(bf16[2,256,1024]{2,1,0:T(8,128)(2,1)} %get-tuple-element.82), channel_id=1, source_target_pairs={{0,16},{8,24},{16,0},{24,8},{1,17},{9,25},{17,1},{25,9},{2,18},{10... | collective-permute-start | bytes 3145736 | tf_op jit(solution)/shard_map/ppermute | solution.py:204
  66.2 8.0 %forward_part.10 = (f32[2,256,1024]{2,1,0:T(8,128)S(1)}, bf16[2,256,1024]{2,1,0:T(8,128)(2,1)}) custom-call(s32[25]{0:T(128)S(1)} %get-tuple-element.65.flags, bf16[512,2048]{1,0:T(8,128)(2,1)S(1)} %copy-done.1, bf16[2048,4096]{1,0:T(8,128)(2,1)} %gate.7, bf16[2048,4096]{1,0:T(8,128)(2,1)} %up.7), custom_call_target="tpu_custom_call" | custom-call | flops 4294967296 | bytes 15728640 | tf_op jit(solution)/shard_map/forward_part/pallas_call | solution.py:61
  75.4 7.9 %forward_part.11 = (f32[2,256,1024]{2,1,0:T(8,128)S(1)}, bf16[2,256,1024]{2,1,0:T(8,128)(2,1)S(1)}) custom-call(s32[25]{0:T(128)S(1)} %get-tuple-element.67.flags, bf16[512,2048]{1,0:T(8,128)(2,1)S(1)} %copy-done.1, bf16[2048,4096]{1,0:T(8,128)(2,1)} %gate.7, bf16[2048,4096]{1,0:T(8,128)(2,1)} %up.7), custom_call_target="tpu_custom_call" | custom-call | flops 4294967296 | bytes 15728640 | tf_op jit(solution)/shard_map/forward_part/pallas_call | solution.py:61
  87.8 6.4 %forward_part.12 = (f32[1,256,1024]{2,1,0:T(8,128)S(1)}, bf16[1,256,1024]{2,1,0:T(8,128)(2,1)S(1)}) custom-call(s32[25]{0:T(128)S(1)} %get-tuple-element.61.flags, bf16[512,2048]{1,0:T(8,128)(2,1)S(1)} %copy-done.3, bf16[4096,2048]{1,0:T(8,128)(2,1)} %refs_0_.15), custom_call_target="tpu_custom_call" | custom-call | flops 2147483648 | bytes 9961472 | tf_op jit(solution)/shard_map/forward_part/pallas_call | solution.py:61
  94.2 6.9 %forward_part.13 = (f32[1,256,1024]{2,1,0:T(8,128)S(1)}, bf16[1,256,1024]{2,1,0:T(8,128)(2,1)S(1)}) custom-call(s32[25]{0:T(128)S(1)} %get-tuple-element.63.flags, bf16[512,2048]{1,0:T(8,128)(2,1)S(1)} %copy-done.3, bf16[4096,2048]{1,0:T(8,128)(2,1)} %refs_0_.15), custom_call_target="tpu_custom_call" | custom-call | flops 2147483648 | bytes 9961472 | tf_op jit(solution)/shard_map/forward_part/pallas_call | solution.py:61
  101.1 7.3 %forward_part.14 = (f32[1,256,1024]{2,1,0:T(8,128)S(1)}, bf16[1,256,1024]{2,1,0:T(8,128)(2,1)S(1)}) custom-call(s32[25]{0:T(128)S(1)} %get-tuple-element.65.flags, bf16[512,2048]{1,0:T(8,128)(2,1)S(1)} %copy-done.3, bf16[4096,2048]{1,0:T(8,128)(2,1)} %refs_0_.15), custom_call_target="tpu_custom_call" | custom-call | flops 2147483648 | bytes 9961472 | tf_op jit(solution)/shard_map/forward_part/pallas_call | solution.py:61
  108.4 6.1 %forward_part.15 = (f32[1,256,1024]{2,1,0:T(8,128)S(1)}, bf16[1,256,1024]{2,1,0:T(8,128)(2,1)S(1)}) custom-call(s32[25]{0:T(128)S(1)} %get-tuple-element.67.flags, bf16[512,2048]{1,0:T(8,128)(2,1)S(1)} %copy-done.3, bf16[4096,2048]{1,0:T(8,128)(2,1)} %refs_0_.15), custom_call_target="tpu_custom_call" | custom-call | flops 2147483648 | bytes 9961472 | tf_op jit(solution)/shard_map/forward_part/pallas_call | solution.py:61
  114.5 1.8 collective-permute-start.16
  118.8 1.7 convert_add_fusion.2
  123.9 1.7 convert_add_fusion.3
  125.6 3.8 %collective-permute-done.16 = bf16[1,256,1024]{2,1,0:T(8,128)(2,1)S(1)} collective-permute-done((bf16[1,256,1024]{2,1,0:T(8,128)(2,1)S(1)}, bf16[1,256,1024]{2,1,0:T(8,128)(2,1)S(1)}, u32[]{:S(2)}, u32[]{:S(2)}) %collective-permute-start.16) | collective-permute-done | bytes 524320 | tf_op jit(solution)/shard_map/ppermute | solution.py:204
  131.8 8.8 %collective-permute-done.6 = bf16[1,256,1024]{2,1,0:T(8,128)(2,1)S(1)} collective-permute-done((bf16[1,256,1024]{2,1,0:T(8,128)(2,1)S(1)}, bf16[1,256,1024]{2,1,0:T(8,128)(2,1)S(1)}, u32[]{:S(2)}, u32[]{:S(2)}) %collective-permute-start.6) | collective-permute-done | bytes 524320 | tf_op jit(solution)/shard_map/ppermute | solution.py:204
  143.1 16.1 %collective-permute-done.17 = bf16[3,128,1024]{2,1,0:T(8,128)(2,1)S(1)} collective-permute-done((bf16[3,128,1024]{2,1,0:T(8,128)(2,1)S(1)}, bf16[3,128,1024]{2,1,0:T(8,128)(2,1)S(1)}, u32[]{:S(2)}, u32[]{:S(2)}) %collective-permute-start.17) | collective-permute-done | bytes 786464 | tf_op jit(solution)/shard_map/ppermute | solution.py:204
  161.5 14.5 %collective-permute-done.7 = bf16[3,128,1024]{2,1,0:T(8,128)(2,1)S(1)} collective-permute-done((bf16[3,128,1024]{2,1,0:T(8,128)(2,1)S(1)}, bf16[3,128,1024]{2,1,0:T(8,128)(2,1)S(1)}, u32[]{:S(2)}, u32[]{:S(2)}) %collective-permute-start.7) | collective-permute-done | bytes 786464 | tf_op jit(solution)/shard_map/ppermute | solution.py:204
  178.4 14.5 %collective-permute-done.18 = bf16[3,128,1024]{2,1,0:T(8,128)(2,1)S(1)} collective-permute-done((bf16[3,128,1024]{2,1,0:T(8,128)(2,1)S(1)}, bf16[3,128,1024]{2,1,0:T(8,128)(2,1)S(1)}, u32[]{:S(2)}, u32[]{:S(2)}) %collective-permute-start.18) | collective-permute-done | bytes 786464 | tf_op jit(solution)/shard_map/ppermute | solution.py:204
  194.5 15.3 %collective-permute-done.8 = bf16[3,128,1024]{2,1,0:T(8,128)(2,1)S(1)} collective-permute-done((bf16[3,128,1024]{2,1,0:T(8,128)(2,1)S(1)}, bf16[3,128,1024]{2,1,0:T(8,128)(2,1)S(1)}, u32[]{:S(2)}, u32[]{:S(2)}) %collective-permute-start.8) | collective-permute-done | bytes 786464 | tf_op jit(solution)/shard_map/ppermute | solution.py:204
  211.4 30.4 %collective-permute-done.19.far = bf16[3,256,1024]{2,1,0:T(8,128)(2,1)S(1)} collective-permute-done((bf16[3,256,1024]{2,1,0:T(8,128)(2,1)S(1)}, bf16[3,256,1024]{2,1,0:T(8,128)(2,1)S(1)}, u32[]{:S(2)}, u32[]{:S(2)}) %collective-permute-start.19) | collective-permute-done | bytes 1572896 | tf_op jit(solution)/shard_map/ppermute | solution.py:204
  241.8 8.2 %input_grad_part.4.refs_0_ = f32[512,2048]{1,0:T(8,128)S(1)} custom-call(s32[25]{0:T(128)S(1)} %get-tuple-element.61.flags, bf16[3,256,1024]{2,1,0:T(8,128)(2,1)S(1)} %pad_maximum_fusion.3.near, bf16[3,256,1024]{2,1,0:T(8,128)(2,1)S(1)} %collective-permute-done.19.far, bf16[2048,4096]{1,0:T(8,128)(2,1)} %gate.7, bf16[2048,4096]{1,0:T(8,128)(2,1)} %up.7), custom_call_target="tpu_custom_call" | custom-call | flops 4294967296 | bytes 16777216 | tf_op jit(solution)/shard_map/input_grad_part/pallas_call | solution.py:107
  250.0 8.4 %input_grad_part.5.refs_0_ = f32[512,2048]{1,0:T(8,128)S(1)} custom-call(s32[25]{0:T(128)S(1)} %get-tuple-element.63.flags, bf16[3,256,1024]{2,1,0:T(8,128)(2,1)S(1)} %pad_maximum_fusion.2.near, bf16[3,256,1024]{2,1,0:T(8,128)(2,1)S(1)} %collective-permute-done.14.far, bf16[2048,4096]{1,0:T(8,128)(2,1)} %gate.7, ...), custom_call_target="tpu_custom_call", output_to_operand_aliasing={{}: (5, {})} | custom-call | flops 4294967296 | bytes 16777216 | tf_op jit(solution)/shard_map/input_grad_part/pallas_call | solution.py:107
  258.4 13.5 %collective-permute-done.9.far = bf16[3,256,1024]{2,1,0:T(8,128)(2,1)S(1)} collective-permute-done((bf16[3,256,1024]{2,1,0:T(8,128)(2,1)S(1)}, bf16[3,256,1024]{2,1,0:T(8,128)(2,1)S(1)}, u32[]{:S(2)}, u32[]{:S(2)}) %collective-permute-start.9) | collective-permute-done | bytes 1572896 | tf_op jit(solution)/shard_map/ppermute | solution.py:204
  271.9 7.5 %input_grad_part.6.refs_0_ = f32[512,2048]{1,0:T(8,128)S(1)} custom-call(s32[25]{0:T(128)S(1)} %get-tuple-element.65.flags, bf16[3,256,1024]{2,1,0:T(8,128)(2,1)S(1)} %pad_maximum_fusion.1.near, bf16[3,256,1024]{2,1,0:T(8,128)(2,1)S(1)} %collective-permute-done.9.far, bf16[2048,4096]{1,0:T(8,128)(2,1)} %gate.7, ...), custom_call_target="tpu_custom_call", output_to_operand_aliasing={{}: (5, {})} | custom-call | flops 4294967296 | bytes 16777216 | tf_op jit(solution)/shard_map/input_grad_part/pallas_call | solution.py:107
  279.4 8.0 %input_grad_part.7 = f32[512,2048]{1,0:T(8,128)S(1)} custom-call(s32[25]{0:T(128)S(1)} %get-tuple-element.67.flags, bf16[3,256,1024]{2,1,0:T(8,128)(2,1)S(1)} %pad_maximum_fusion.near, bf16[3,256,1024]{2,1,0:T(8,128)(2,1)S(1)} %collective-permute-done.4.far, bf16[2048,4096]{1,0:T(8,128)(2,1)} %gate.7, ...), custom_call_target="tpu_custom_call", output_to_operand_aliasing={{}: (5, {})} | custom-call | flops 4294967296 | bytes 16777216 | tf_op jit(solution)/shard_map/input_grad_part/pallas_call | solution.py:107
  287.4 2.0 copy-done
  296.6 9.1 %weight_grad_part.4 = (bf16[2048,4096]{1,0:T(8,128)(2,1)}, bf16[2048,4096]{1,0:T(8,128)(2,1)}, bf16[4096,2048]{1,0:T(8,128)(2,1)}) custom-call(s32[25]{0:T(128)S(1)} %get-tuple-element.61.flags, bf16[3,256,1024]{2,1,0:T(8,128)(2,1)S(1)} %copy-done.12, bf16[3,256,1024]{2,1,0:T(8,128)(2,1)S(1)} %copy-done.26, bf16[512,2048]{1,0:T(8,128)(2,1)S(1)} %copy-done.2, ...), custom_call_target="tpu_custom_call" | custom-call | flops 6442450944 | bytes 16777216 | tf_op jit(solution)/shard_map/weight_grad_part/pallas_call | solution.py:160
  305.6 8.6 %weight_grad_part.5 = (bf16[2048,4096]{1,0:T(8,128)(2,1)}, bf16[2048,4096]{1,0:T(8,128)(2,1)}, bf16[4096,2048]{1,0:T(8,128)(2,1)}) custom-call(s32[25]{0:T(128)S(1)} %get-tuple-element.63.flags, bf16[3,256,1024]{2,1,0:T(8,128)(2,1)S(1)} %copy-done.6, ...), custom_call_target="tpu_custom_call", output_to_operand_aliasing={{0}: (5, {}), {1}: (6, {}), {2}: (7, {})} | custom-call | flops 6442450944 | bytes 16777216 | tf_op jit(solution)/shard_map/weight_grad_part/pallas_call | solution.py:160
  314.3 8.4 %weight_grad_part.6 = (bf16[2048,4096]{1,0:T(8,128)(2,1)}, bf16[2048,4096]{1,0:T(8,128)(2,1)}, bf16[4096,2048]{1,0:T(8,128)(2,1)}) custom-call(s32[25]{0:T(128)S(1)} %get-tuple-element.65.flags, bf16[3,256,1024]{2,1,0:T(8,128)(2,1)S(1)} %copy-done.8, ...), custom_call_target="tpu_custom_call", output_to_operand_aliasing={{0}: (5, {}), {1}: (6, {}), {2}: (7, {})} | custom-call | flops 6442450944 | bytes 16777216 | tf_op jit(solution)/shard_map/weight_grad_part/pallas_call | solution.py:160
  322.7 7.7 %weight_grad_part.7 = (bf16[2048,4096]{1,0:T(8,128)(2,1)}, bf16[2048,4096]{1,0:T(8,128)(2,1)}, bf16[4096,2048]{1,0:T(8,128)(2,1)}) custom-call(s32[25]{0:T(128)S(1)} %get-tuple-element.67.flags, bf16[3,256,1024]{2,1,0:T(8,128)(2,1)S(1)} %copy-done.10, ...), custom_call_target="tpu_custom_call", output_to_operand_aliasing={{0}: (5, {}), {1}: (6, {}), {2}: (7, {})} | custom-call | flops 6442450944 | bytes 16777216 | tf_op jit(solution)/shard_map/weight_grad_part/pallas_call | solution.py:160
  330.4 11.4 %reduce-scatter.2.cloned.1.call-done = f32[64,2048]{1,0:T(8,128)} async-done(((f32[512,2048]{1,0:T(8,128)}), f32[64,2048]{1,0:T(8,128)}) %reduce-scatter.2.cloned.1.call-update) | async-done | bytes 524304 | tf_op jit(solution)/shard_map/reduce_scatter | solution.py:274
  341.7 1.8 convert_element_type.103
  (135 shorter events, 36.5 us)
Async XLA Ops:
  7.2 34.3 %all-gather.3.cloned.1.call-start = ((), (), s32[]{:S(2)}) async-start(), calls=%async_computation.1 | async-start | bytes 2359296 | tf_op jit(solution)/shard_map/all_gather | solution.py:252
  7.9 78.3 %all-gather.5.cloned.1.call-start = ((), (), s32[]{:S(2)}) async-start(), calls=%async_computation.2 | async-start | bytes 2359296 | tf_op jit(solution)/shard_map/all_gather | solution.py:253
  8.6 333.1 %reduce-scatter.2.cloned.1.call-start = ((), (), s32[]{:S(2)}) async-start(), calls=%async_computation.3 | async-start | bytes 4718592 | tf_op jit(solution)/shard_map/reduce_scatter | solution.py:274
  52.4 9.8 %copy-start.19 = (f32[2,256,1024]{2,1,0:T(8,128)}, f32[2,256,1024]{2,1,0:T(8,128)S(1)}, u32[]{:S(2)}) copy-start(f32[2,256,1024]{2,1,0:T(8,128)S(1)} %get-tuple-element.90) | copy-start | bytes 6291460
  52.4 62.1 %collective-permute-start.15 = (bf16[2,256,1024]{2,1,0:T(8,128)(2,1)}, bf16[2,256,1024]{2,1,0:T(8,128)(2,1)}, u32[]{:S(2)}, u32[]{:S(2)}) collective-permute-start(bf16[2,256,1024]{2,1,0:T(8,128)(2,1)} %get-tuple-element.88), channel_id=1, source_target_pairs={{0,8},{8,0},{16,24},{24,16},{1,9},{9,1},{17,25},{25,17},{2,10},{10... | collective-permute-start | bytes 3145736 | tf_op jit(solution)/shard_map/ppermute | solution.py:204
  62.2 54.1 %collective-permute-start.10 = (bf16[2,256,1024]{2,1,0:T(8,128)(2,1)}, bf16[2,256,1024]{2,1,0:T(8,128)(2,1)}, u32[]{:S(2)}, u32[]{:S(2)}) collective-permute-start(bf16[2,256,1024]{2,1,0:T(8,128)(2,1)} %get-tuple-element.82), channel_id=1, source_target_pairs={{0,16},{8,24},{16,0},{24,8},{1,17},{9,25},{17,1},{25,9},{2,18},{10... | collective-permute-start | bytes 3145736 | tf_op jit(solution)/shard_map/ppermute | solution.py:204
  75.4 40.8 %collective-permute-start.5 = (bf16[2,256,1024]{2,1,0:T(8,128)(2,1)}, bf16[2,256,1024]{2,1,0:T(8,128)(2,1)}, u32[]{:S(2)}, u32[]{:S(2)}) collective-permute-start(bf16[2,256,1024]{2,1,0:T(8,128)(2,1)} %get-tuple-element.76), channel_id=1, source_target_pairs={{0,8},{8,0},{16,24},{24,16},{1,9},{9,1},{17,25},{25,17},{2,10},{10... | collective-permute-start | bytes 3145736 | tf_op jit(solution)/shard_map/ppermute | solution.py:204
  84.6 36.0 %collective-permute-start = (bf16[2,256,1024]{2,1,0:T(8,128)(2,1)S(1)}, bf16[2,256,1024]{2,1,0:T(8,128)(2,1)}, u32[]{:S(2)}, u32[]{:S(2)}) collective-permute-start(bf16[2,256,1024]{2,1,0:T(8,128)(2,1)S(1)} %get-tuple-element.70), channel_id=1, source_target_pairs={{0,16},{8,24},{16,0},{24,8},{1,17},{9,25},{17,1},{25,9},{2,18},{10... | collective-permute-start | bytes 3145736 | tf_op jit(solution)/shard_map/ppermute | solution.py:204
  108.4 8.8 %copy-start.20 = (f32[2,256,1024]{2,1,0:T(8,128)S(1)}, f32[2,256,1024]{2,1,0:T(8,128)}, u32[]{:S(2)}) copy-start(f32[2,256,1024]{2,1,0:T(8,128)} %copy-done.19) | copy-start | bytes 6291460
  114.5 14.9 %collective-permute-start.16 = (bf16[1,256,1024]{2,1,0:T(8,128)(2,1)S(1)}, bf16[1,256,1024]{2,1,0:T(8,128)(2,1)S(1)}, u32[]{:S(2)}, u32[]{:S(2)}) collective-permute-start(bf16[1,256,1024]{2,1,0:T(8,128)(2,1)S(1)} %get-tuple-element.89), channel_id=1, source_target_pairs={{0,8},{8,0},{16,24},{24,16},{1,9},{9,1},{17,25},{25,17},{2,10},{10... | collective-permute-start | bytes 1572872 | tf_op jit(solution)/shard_map/ppermute | solution.py:204
  116.3 14.9 %collective-permute-start.11 = (bf16[1,256,1024]{2,1,0:T(8,128)(2,1)S(1)}, bf16[1,256,1024]{2,1,0:T(8,128)(2,1)S(1)}, u32[]{:S(2)}, u32[]{:S(2)}) collective-permute-start(bf16[1,256,1024]{2,1,0:T(8,128)(2,1)S(1)} %get-tuple-element.83), channel_id=1, source_target_pairs={{0,16},{8,24},{16,0},{24,8},{1,17},{9,25},{17,1},{25,9},{2,18},{10... | collective-permute-start | bytes 1572872 | tf_op jit(solution)/shard_map/ppermute | solution.py:204
  116.3 24.4 %collective-permute-start.6 = (bf16[1,256,1024]{2,1,0:T(8,128)(2,1)S(1)}, bf16[1,256,1024]{2,1,0:T(8,128)(2,1)S(1)}, u32[]{:S(2)}, u32[]{:S(2)}) collective-permute-start(bf16[1,256,1024]{2,1,0:T(8,128)(2,1)S(1)} %get-tuple-element.77), channel_id=1, source_target_pairs={{0,8},{8,0},{16,24},{24,16},{1,9},{9,1},{17,25},{25,17},{2,10},{10... | collective-permute-start | bytes 1572872 | tf_op jit(solution)/shard_map/ppermute | solution.py:204
  120.6 21.8 %collective-permute-start.1 = (bf16[1,256,1024]{2,1,0:T(8,128)(2,1)S(1)}, bf16[1,256,1024]{2,1,0:T(8,128)(2,1)S(1)}, u32[]{:S(2)}, u32[]{:S(2)}) collective-permute-start(bf16[1,256,1024]{2,1,0:T(8,128)(2,1)S(1)} %get-tuple-element.71), channel_id=1, source_target_pairs={{0,16},{8,24},{16,0},{24,8},{1,17},{9,25},{17,1},{25,9},{2,18},{10... | collective-permute-start | bytes 1572872 | tf_op jit(solution)/shard_map/ppermute | solution.py:204
  129.7 29.5 %collective-permute-start.17 = (bf16[3,128,1024]{2,1,0:T(8,128)(2,1)S(1)}, bf16[3,128,1024]{2,1,0:T(8,128)(2,1)S(1)}, u32[]{:S(2)}, u32[]{:S(2)}) collective-permute-start(bf16[3,128,1024]{2,1,0:T(8,128)(2,1)S(1)} %pad_maximum_fusion.10), channel_id=1, source_target_pairs={{0,16},{8,24},{16,0},{24,8},{1,17},{9,25},{17,1},{25,9},{2,18},{10... | collective-permute-start | bytes 2359304 | tf_op jit(solution)/shard_map/ppermute | solution.py:204
  131.4 28.5 %collective-permute-start.12 = (bf16[3,128,1024]{2,1,0:T(8,128)(2,1)S(1)}, bf16[3,128,1024]{2,1,0:T(8,128)(2,1)S(1)}, u32[]{:S(2)}, u32[]{:S(2)}) collective-permute-start(bf16[3,128,1024]{2,1,0:T(8,128)(2,1)S(1)} %pad_maximum_fusion.8), channel_id=1, source_target_pairs={{0,8},{8,0},{16,24},{24,16},{1,9},{9,1},{17,25},{25,17},{2,10},{10... | collective-permute-start | bytes 2359304 | tf_op jit(solution)/shard_map/ppermute | solution.py:204
  140.9 35.1 %collective-permute-start.7 = (bf16[3,128,1024]{2,1,0:T(8,128)(2,1)S(1)}, bf16[3,128,1024]{2,1,0:T(8,128)(2,1)S(1)}, u32[]{:S(2)}, u32[]{:S(2)}) collective-permute-start(bf16[3,128,1024]{2,1,0:T(8,128)(2,1)S(1)} %pad_maximum_fusion.6), channel_id=1, source_target_pairs={{0,16},{8,24},{16,0},{24,8},{1,17},{9,25},{17,1},{25,9},{2,18},{10... | collective-permute-start | bytes 2359304 | tf_op jit(solution)/shard_map/ppermute | solution.py:204
  142.6 34.1 %collective-permute-start.2 = (bf16[3,128,1024]{2,1,0:T(8,128)(2,1)S(1)}, bf16[3,128,1024]{2,1,0:T(8,128)(2,1)S(1)}, u32[]{:S(2)}, u32[]{:S(2)}) collective-permute-start(bf16[3,128,1024]{2,1,0:T(8,128)(2,1)S(1)} %pad_maximum_fusion.4), channel_id=1, source_target_pairs={{0,8},{8,0},{16,24},{24,16},{1,9},{9,1},{17,25},{25,17},{2,10},{10... | collective-permute-start | bytes 2359304 | tf_op jit(solution)/shard_map/ppermute | solution.py:204
  159.9 33.1 %collective-permute-start.18 = (bf16[3,128,1024]{2,1,0:T(8,128)(2,1)S(1)}, bf16[3,128,1024]{2,1,0:T(8,128)(2,1)S(1)}, u32[]{:S(2)}, u32[]{:S(2)}) collective-permute-start(bf16[3,128,1024]{2,1,0:T(8,128)(2,1)S(1)} %pad_maximum_fusion.11), channel_id=1, source_target_pairs={{0,16},{8,24},{16,0},{24,8},{1,17},{9,25},{17,1},{25,9},{2,18},{10... | collective-permute-start | bytes 2359304 | tf_op jit(solution)/shard_map/ppermute | solution.py:204
  160.6 33.0 %collective-permute-start.13 = (bf16[3,128,1024]{2,1,0:T(8,128)(2,1)S(1)}, bf16[3,128,1024]{2,1,0:T(8,128)(2,1)S(1)}, u32[]{:S(2)}, u32[]{:S(2)}) collective-permute-start(bf16[3,128,1024]{2,1,0:T(8,128)(2,1)S(1)} %pad_maximum_fusion.9), channel_id=1, source_target_pairs={{0,8},{8,0},{16,24},{24,16},{1,9},{9,1},{17,25},{25,17},{2,10},{10... | collective-permute-start | bytes 2359304 | tf_op jit(solution)/shard_map/ppermute | solution.py:204
  176.7 33.1 %collective-permute-start.8 = (bf16[3,128,1024]{2,1,0:T(8,128)(2,1)S(1)}, bf16[3,128,1024]{2,1,0:T(8,128)(2,1)S(1)}, u32[]{:S(2)}, u32[]{:S(2)}) collective-permute-start(bf16[3,128,1024]{2,1,0:T(8,128)(2,1)S(1)} %pad_maximum_fusion.7), channel_id=1, source_target_pairs={{0,16},{8,24},{16,0},{24,8},{1,17},{9,25},{17,1},{25,9},{2,18},{10... | collective-permute-start | bytes 2359304 | tf_op jit(solution)/shard_map/ppermute | solution.py:204
  177.4 33.0 %collective-permute-start.3 = (bf16[3,128,1024]{2,1,0:T(8,128)(2,1)S(1)}, bf16[3,128,1024]{2,1,0:T(8,128)(2,1)S(1)}, u32[]{:S(2)}, u32[]{:S(2)}) collective-permute-start(bf16[3,128,1024]{2,1,0:T(8,128)(2,1)S(1)} %pad_maximum_fusion.5), channel_id=1, source_target_pairs={{0,8},{8,0},{16,24},{24,16},{1,9},{9,1},{17,25},{25,17},{2,10},{10... | collective-permute-start | bytes 2359304 | tf_op jit(solution)/shard_map/ppermute | solution.py:204
  193.2 48.6 %copy-start.11 = (bf16[3,256,1024]{2,1,0:T(8,128)(2,1)}, bf16[3,256,1024]{2,1,0:T(8,128)(2,1)S(1)}, u32[]{:S(2)}) copy-start(bf16[3,256,1024]{2,1,0:T(8,128)(2,1)S(1)} %pad_maximum_fusion.3.near) | copy-start | bytes 4718596
  193.2 48.6 %collective-permute-start.19 = (bf16[3,256,1024]{2,1,0:T(8,128)(2,1)S(1)}, bf16[3,256,1024]{2,1,0:T(8,128)(2,1)S(1)}, u32[]{:S(2)}, u32[]{:S(2)}) collective-permute-start(bf16[3,256,1024]{2,1,0:T(8,128)(2,1)S(1)} %pad_maximum_fusion.3.near), channel_id=1, source_target_pairs={{0,8},{8,0},{16,24},{24,16},{1,9},{9,1},{17,25},{25,17},{2,10},{10... | collective-permute-start | bytes 4718600 | tf_op jit(solution)/shard_map/ppermute | solution.py:204
  193.8 56.1 %copy-start.5 = (bf16[3,256,1024]{2,1,0:T(8,128)(2,1)}, bf16[3,256,1024]{2,1,0:T(8,128)(2,1)S(1)}, u32[]{:S(2)}) copy-start(bf16[3,256,1024]{2,1,0:T(8,128)(2,1)S(1)} %pad_maximum_fusion.2.near) | copy-start | bytes 4718596
  193.8 56.1 %collective-permute-start.14 = (bf16[3,256,1024]{2,1,0:T(8,128)(2,1)S(1)}, bf16[3,256,1024]{2,1,0:T(8,128)(2,1)S(1)}, u32[]{:S(2)}, u32[]{:S(2)}) collective-permute-start(bf16[3,256,1024]{2,1,0:T(8,128)(2,1)S(1)} %pad_maximum_fusion.2.near), channel_id=1, source_target_pairs={{0,16},{8,24},{16,0},{24,8},{1,17},{9,25},{17,1},{25,9},{2,18},{10... | collective-permute-start | bytes 4718600 | tf_op jit(solution)/shard_map/ppermute | solution.py:204
  210.0 61.9 %copy-start.7 = (bf16[3,256,1024]{2,1,0:T(8,128)(2,1)}, bf16[3,256,1024]{2,1,0:T(8,128)(2,1)S(1)}, u32[]{:S(2)}) copy-start(bf16[3,256,1024]{2,1,0:T(8,128)(2,1)S(1)} %pad_maximum_fusion.1.near) | copy-start | bytes 4718596
  210.0 61.9 %collective-permute-start.9 = (bf16[3,256,1024]{2,1,0:T(8,128)(2,1)S(1)}, bf16[3,256,1024]{2,1,0:T(8,128)(2,1)S(1)}, u32[]{:S(2)}, u32[]{:S(2)}) collective-permute-start(bf16[3,256,1024]{2,1,0:T(8,128)(2,1)S(1)} %pad_maximum_fusion.1.near), channel_id=1, source_target_pairs={{0,8},{8,0},{16,24},{24,16},{1,9},{9,1},{17,25},{25,17},{2,10},{10... | collective-permute-start | bytes 4718600 | tf_op jit(solution)/shard_map/ppermute | solution.py:204
  210.7 68.8 %copy-start.9 = (bf16[3,256,1024]{2,1,0:T(8,128)(2,1)}, bf16[3,256,1024]{2,1,0:T(8,128)(2,1)S(1)}, u32[]{:S(2)}) copy-start(bf16[3,256,1024]{2,1,0:T(8,128)(2,1)S(1)} %pad_maximum_fusion.near) | copy-start | bytes 4718596
  210.7 68.7 %collective-permute-start.4 = (bf16[3,256,1024]{2,1,0:T(8,128)(2,1)S(1)}, bf16[3,256,1024]{2,1,0:T(8,128)(2,1)S(1)}, u32[]{:S(2)}, u32[]{:S(2)}) collective-permute-start(bf16[3,256,1024]{2,1,0:T(8,128)(2,1)S(1)} %pad_maximum_fusion.near), channel_id=1, source_target_pairs={{0,16},{8,24},{16,0},{24,8},{1,17},{9,25},{17,1},{25,9},{2,18},{10... | collective-permute-start | bytes 4718600 | tf_op jit(solution)/shard_map/ppermute | solution.py:204
  296.6 9.1 %copy-start.6 = (bf16[3,256,1024]{2,1,0:T(8,128)(2,1)S(1)}, bf16[3,256,1024]{2,1,0:T(8,128)(2,1)}, u32[]{:S(2)}) copy-start(bf16[3,256,1024]{2,1,0:T(8,128)(2,1)} %copy-done.5) | copy-start | bytes 4718596
  296.6 9.1 %copy-start.14 = (bf16[3,256,1024]{2,1,0:T(8,128)(2,1)S(1)}, bf16[3,256,1024]{2,1,0:T(8,128)(2,1)}, u32[]{:S(2)}) copy-start(bf16[3,256,1024]{2,1,0:T(8,128)(2,1)} %copy-done.13) | copy-start | bytes 4718596
  305.6 8.6 %copy-start.8 = (bf16[3,256,1024]{2,1,0:T(8,128)(2,1)S(1)}, bf16[3,256,1024]{2,1,0:T(8,128)(2,1)}, u32[]{:S(2)}) copy-start(bf16[3,256,1024]{2,1,0:T(8,128)(2,1)} %copy-done.7) | copy-start | bytes 4718596
  (18 other events, 70.3 us)
Sparse Core Ops, SparseCore 0:
  9.6 31.7 all-gather.2
  43.0 28.5 all-gather.4
  290.7 50.9 reduce-scatter.1
where the time goes:
time: 351 us; the launch traced here: 350 us
  waiting for transfers between devices  162 us (46%)
  Pallas kernels  127 us (36%)
  starting transfers between devices  17 us (5%)
  local copies, waits for them, and re-layouts  16.7 us (5%)
  between operations  14.4 us (4%)
  other arithmetic  12.7 us (4%)
    ppermute x20, waiting for transfers between devices, swap(): return lax.ppermute(part, 'row', [(i, i ^ 1 << bit) for i in range(rows)])  118 us
    pallas_call x8, Pallas kernels, forward(): pl.pallas_call(functools.partial(forward_kernel, kinds=kinds), grid_spec=...  60.9 us
    pallas_call x4, Pallas kernels, weight_grads(): pl.pallas_call(weight_kernel, grid_spec=pltpu.PrefetchScalarGridSpec(num_...  33.8 us
    pallas_call x4, Pallas kernels, add_input_grad(): pl.pallas_call(input_kernel, grid_spec=pltpu.PrefetchScalarGridSpec(num_s...  32 us
    all_gather x1, waiting for transfers between devices, shards(): tokens_all = lax.all_gather(tokens, 'col', axis=0, tiled=True)  31.3 us
    ppermute x20, starting transfers between devices, swap(): return lax.ppermute(part, 'row', [(i, i ^ 1 << bit) for i in range(rows)])  16.9 us
    unnamed x54, local copies, waits for them, and re-layouts  15 us
    reduce_scatter x1, waiting for transfers between devices, shards(): input_grad = lax.psum_scatter(total, 'col', scatter_dimension=0, tiled=True)  11.4 us
  transfers between devices with their start and end apart: 23, of which 12 were waited for; matrix products, arithmetic and copies ran while one was open for 4% of the time, Pallas kernels for 34%

commit v1 on v0

--- a/solution.py
+++ b/solution.py
@@ -78,50 +78,45 @@
     )(flags, acts, *weights)
 
 
-def input_kernel(flags, near, far, gate, up, *refs):
-    acc = refs[-1]
+def input_kernel(flags, delta, gate, up, acc_in, acc):
     step, inner = pl.program_id(0), pl.program_id(1)
     steps, group = pl.num_programs(0), pl.num_programs(1)
 
     @pl.when(inner == 0)
     def _():
-        acc[...] = refs[0][...] if len(refs) == 2 else jnp.zeros_like(acc)
-
-    half = near.shape[1]
+        acc[...] = acc_in[...]
+
     for kind, weight in ((0, gate), (1, up)):
 
         @pl.when(flags[1 + (kind * steps + step) * group + inner] != 0)
         def _(kind=kind, weight=weight):
-            for delta, place in ((near, flags[0]), (far, 1 - flags[0])):
-                rows = pl.ds(pl.multiple_of(place * half, half), half)
-                acc[rows, :] += dot(delta[kind], weight[...], NT)
-
-
-def add_input_grad(flags, near, far, gate_weight, up_weight, total, start, group):
-    half = near.shape[1]
-    tokens, width = 2 * half, gate_weight.shape[0]
+            acc[...] += dot(delta[kind], weight[...], NT)
+
+
+def add_input_grad(flags, delta, near, gate_weight, up_weight, total, start, group):
+    half = delta.shape[1]
+    tokens, width = total.shape
     delta_spec = pl.BlockSpec((2, half, BLK), lambda d, j, f: (0, 0, j))
     weight_spec = pl.BlockSpec((BLK, BLK), lambda d, j, f: (d, start + j))
-    acc_spec = pl.BlockSpec((tokens, BLK), lambda d, j, f: (0, d))
-    first = total is None
+    acc_spec = pl.BlockSpec((half, BLK), lambda d, j, f: (f[0] if near else 1 - f[0], d))
     return pl.pallas_call(
         input_kernel,
         grid_spec=pltpu.PrefetchScalarGridSpec(
             num_scalar_prefetch=1,
             grid=(width // BLK, group),
-            in_specs=[delta_spec] * 2 + [weight_spec] * 2 + ([] if first else [acc_spec]),
+            in_specs=[delta_spec] + [weight_spec] * 2 + [acc_spec],
             out_specs=acc_spec,
         ),
         out_shape=jax.ShapeDtypeStruct((tokens, width), jnp.float32),
-        input_output_aliases={} if first else {5: 0},
+        input_output_aliases={4: 0},
         compiler_params=pltpu.CompilerParams(vmem_limit_bytes=VMEM_LIMIT),
         cost_estimate=pl.CostEstimate(
-            flops=4 * tokens * width * BLK * group,
-            bytes_accessed=4 * width * BLK * group + 8 * tokens * width,
+            flops=4 * half * width * BLK * group,
+            bytes_accessed=4 * width * BLK * group + 8 * half * width,
             transcendentals=0,
         ),
         name="input_grad_part",
-    )(flags, near, far, gate_weight, up_weight, *([] if first else [total]))
+    )(flags, delta, gate_weight, up_weight, total)
 
 
 def weight_kernel(flags, near, far, tokens, cotan, *refs):
@@ -209,8 +204,7 @@
     def after(value, earlier):
         return lax.optimization_barrier((value, earlier))
 
-    def finish_sum(value, slope, order):
-        got = swap(value[1], order[0])
+    def finish_sum(value, slope, got, order):
         give, got = after(slope[1], got)
         parts = [
             value[0] + got.astype(jnp.float32),
@@ -257,20 +251,32 @@
         (tokens_all, [gate_weight, up_weight], (0, 1), values),
         (cotan_all, [down_weight], (2,), slopes),
     ):
+        arrived = [swap(value[1], order[0]) for value, order in zip(values, orders)]
         for g in range(groups):
             order_flags = flags[g]
             if last is not None:
                 order_flags, last[0] = after(order_flags, last[0])
+            if arrived and g > 0:
+                order_flags, arrived[g - 1] = after(order_flags, arrived[g - 1])
             last = list(forward(order_flags, acts, weights, kinds, g * group, group, wire))
             results.append(last)
-    total, halves = None, []
+    halves = []
     for g in range(groups):
-        pair, slope = finish_sum(values[g], slopes[g], orders[g])
-        near, far = spread(swiglu(pair[0], pair[1], slope[0]), orders[g])
-        halves.append((near, far))
-        total = add_input_grad(
-            flags[g], near, far, gate_weight, up_weight, total, g * group, group
-        )
+        pair, slope = finish_sum(values[g], slopes[g], arrived[g], orders[g])
+        halves.append(spread(swiglu(pair[0], pair[1], slope[0]), orders[g]))
+    total = jnp.zeros(tokens_all.shape, jnp.float32)
+    for place in range(2):
+        for g in range(groups):
+            total = add_input_grad(
+                flags[g],
+                halves[g][place],
+                place == 0,
+                gate_weight,
+                up_weight,
+                total,
+                g * group,
+                group,
+            )
     input_grad = lax.psum_scatter(total, "col", scatter_dimension=0, tiled=True)
     grads = None
     for g, (near, far) in enumerate(halves):

time: 351 us -> 366 us (1.043)
  Pallas kernels: 127 us -> 147 us
  waiting for transfers between devices: 162 us -> 149 us
  starting transfers between devices: 17 us -> 21 us
    pallas_call x4 -> x8, Pallas kernels: 32 us -> 56.9 us  [add_input_grad(): pl.pallas_call(input_kernel, grid_spec=pltpu.PrefetchScalarGridSpec(num_s...]
    ppermute x20, waiting for transfers between devices: 118 us -> 102 us  [swap(): return lax.ppermute(part, 'row', [(i, i ^ 1 << bit) for i in range(rows)])]
    ppermute x20, starting transfers between devices: 16.9 us -> 20.9 us  [swap(): return lax.ppermute(part, 'row', [(i, i ^ 1 << bit) for i in range(rows)])]
    unnamed x54 -> x58, local copies, waits for them, and re-layouts: 15 us -> 16.1 us
  transfers between devices with their start and end apart: 23 -> 23, of which waited for: 12 -> 8; matrix products, arithmetic and copies ran while one was open for 4% -> 4% of each run, Pallas kernels for 34% -> 38%
where the time goes in v1:
time: 366 us; the launch traced here: 364 us
  waiting for transfers between devices  149 us (41%)
  Pallas kernels  147 us (40%)
  starting transfers between devices  21 us (6%)
  local copies, waits for them, and re-layouts  18.3 us (5%)
  other arithmetic  14.8 us (4%)
  between operations  14.5 us (4%)
    ppermute x20, waiting for transfers between devices, swap(): return lax.ppermute(part, 'row', [(i, i ^ 1 << bit) for i in range(rows)])  102 us
    pallas_call x8, Pallas kernels, forward(): pl.pallas_call(functools.partial(forward_kernel, kinds=kinds), grid_spec=...  58.4 us
    pallas_call x8, Pallas kernels, add_input_grad(): pl.pallas_call(input_kernel, grid_spec=pltpu.PrefetchScalarGridSpec(num_s...  56.9 us
    pallas_call x4, Pallas kernels, weight_grads(): pl.pallas_call(weight_kernel, grid_spec=pltpu.PrefetchScalarGridSpec(num_...  31.3 us
    all_gather x1, waiting for transfers between devices, shards(): tokens_all = lax.all_gather(tokens, 'col', axis=0, tiled=True)  31.3 us
    ppermute x20, starting transfers between devices, swap(): return lax.ppermute(part, 'row', [(i, i ^ 1 << bit) for i in range(rows)])  20.9 us
    unnamed x58, local copies, waits for them, and re-layouts  16.1 us
    reduce_scatter x1, waiting for transfers between devices, shards(): input_grad = lax.psum_scatter(total, 'col', scatter_dimension=0, tiled=True)  13.9 us
  transfers between devices with their start and end apart: 23, of which 8 were waited for; matrix products, arithmetic and copies ran while one was open for 4% of the time, Pallas kernels for 38%

profile of v1, /device:TPU:0, one launch (start us, length us, event | category | flops | bytes accessed | tf_op | source)
XLA Modules:
  0.0 364.3 jit_solution(13767341567629996552)
XLA Ops:
  10.1 31.3 %all-gather.3.cloned.1.call-done.acts.tokens = bf16[512,2048]{1,0:T(8,128)(2,1)} async-done(((bf16[64,2048]{1,0:T(8,128)(2,1)}), bf16[512,2048]{1,0:T(8,128)(2,1)}) %all-gather.3.cloned.1.call-update) | async-done | bytes 2097168 | tf_op jit(solution)/shard_map/all_gather | solution.py:246
  43.0 8.5 %forward_part.8 = (f32[2,256,1024]{2,1,0:T(8,128)S(1)}, bf16[2,256,1024]{2,1,0:T(8,128)(2,1)}) custom-call(s32[25]{0:T(128)S(1)} %get-tuple-element.67.flags, bf16[512,2048]{1,0:T(8,128)(2,1)S(1)} %copy-done.1, bf16[2048,4096]{1,0:T(8,128)(2,1)} %gate.15, bf16[2048,4096]{1,0:T(8,128)(2,1)} %up.15), custom_call_target="tpu_custom_call" | custom-call | flops 4294967296 | bytes 15728640 | tf_op jit(solution)/shard_map/forward_part/pallas_call | solution.py:61
  52.8 2.6 collective-permute-start
  55.4 8.5 %forward_part.9 = (f32[2,256,1024]{2,1,0:T(8,128)S(1)}, bf16[2,256,1024]{2,1,0:T(8,128)(2,1)}) custom-call(s32[25]{0:T(128)S(1)} %get-tuple-element.71.flags, bf16[512,2048]{1,0:T(8,128)(2,1)S(1)} %copy-done.1, bf16[2048,4096]{1,0:T(8,128)(2,1)} %gate.15, bf16[2048,4096]{1,0:T(8,128)(2,1)} %up.15), custom_call_target="tpu_custom_call" | custom-call | flops 4294967296 | bytes 15728640 | tf_op jit(solution)/shard_map/forward_part/pallas_call | solution.py:61
  65.5 7.5 %forward_part.10 = (f32[2,256,1024]{2,1,0:T(8,128)S(1)}, bf16[2,256,1024]{2,1,0:T(8,128)(2,1)S(1)}) custom-call(s32[25]{0:T(128)S(1)} %get-tuple-element.75.flags, bf16[512,2048]{1,0:T(8,128)(2,1)S(1)} %copy-done.1, bf16[2048,4096]{1,0:T(8,128)(2,1)} %gate.15, bf16[2048,4096]{1,0:T(8,128)(2,1)} %up.15), custom_call_target="tpu_custom_call" | custom-call | flops 4294967296 | bytes 15728640 | tf_op jit(solution)/shard_map/forward_part/pallas_call | solution.py:61
  74.3 2.5 collective-permute-start.2
  76.8 8.9 %forward_part.11 = (f32[2,256,1024]{2,1,0:T(8,128)S(1)}, bf16[2,256,1024]{2,1,0:T(8,128)(2,1)}) custom-call(s32[25]{0:T(128)S(1)} %get-tuple-element.79.flags, bf16[512,2048]{1,0:T(8,128)(2,1)S(1)} %copy-done.2, bf16[2048,4096]{1,0:T(8,128)(2,1)} %gate.15, bf16[2048,4096]{1,0:T(8,128)(2,1)} %up.15), custom_call_target="tpu_custom_call" | custom-call | flops 4294967296 | bytes 15728640 | tf_op jit(solution)/shard_map/forward_part/pallas_call | solution.py:61
  88.6 6.5 %forward_part.12 = (f32[1,256,1024]{2,1,0:T(8,128)S(1)}, bf16[1,256,1024]{2,1,0:T(8,128)(2,1)S(1)}) custom-call(s32[25]{0:T(128)S(1)} %get-tuple-element.67.flags, bf16[512,2048]{1,0:T(8,128)(2,1)S(1)} %copy-done.3, bf16[4096,2048]{1,0:T(8,128)(2,1)} %refs_0_.15), custom_call_target="tpu_custom_call" | custom-call | flops 2147483648 | bytes 9961472 | tf_op jit(solution)/shard_map/forward_part/pallas_call | solution.py:61
  96.1 6.0 %forward_part.13 = (f32[1,256,1024]{2,1,0:T(8,128)S(1)}, bf16[1,256,1024]{2,1,0:T(8,128)(2,1)S(1)}) custom-call(s32[25]{0:T(128)S(1)} %get-tuple-element.71.flags, bf16[512,2048]{1,0:T(8,128)(2,1)S(1)} %copy-done.3, bf16[4096,2048]{1,0:T(8,128)(2,1)} %refs_0_.15), custom_call_target="tpu_custom_call" | custom-call | flops 2147483648 | bytes 9961472 | tf_op jit(solution)/shard_map/forward_part/pallas_call | solution.py:61
  102.1 2.7 collective-permute-start.12
  104.8 6.5 %forward_part.14 = (f32[1,256,1024]{2,1,0:T(8,128)S(1)}, bf16[1,256,1024]{2,1,0:T(8,128)(2,1)S(1)}) custom-call(s32[25]{0:T(128)S(1)} %get-tuple-element.75.flags, bf16[512,2048]{1,0:T(8,128)(2,1)S(1)} %copy-done.3, bf16[4096,2048]{1,0:T(8,128)(2,1)} %refs_0_.15), custom_call_target="tpu_custom_call" | custom-call | flops 2147483648 | bytes 9961472 | tf_op jit(solution)/shard_map/forward_part/pallas_call | solution.py:61
  115.0 6.1 %forward_part.15 = (f32[1,256,1024]{2,1,0:T(8,128)S(1)}, bf16[1,256,1024]{2,1,0:T(8,128)(2,1)S(1)}) custom-call(s32[25]{0:T(128)S(1)} %get-tuple-element.79.flags, bf16[512,2048]{1,0:T(8,128)(2,1)S(1)} %copy-done.3, bf16[4096,2048]{1,0:T(8,128)(2,1)} %refs_0_.15), custom_call_target="tpu_custom_call" | custom-call | flops 2147483648 | bytes 9961472 | tf_op jit(solution)/shard_map/forward_part/pallas_call | solution.py:61
  129.1 2.0 collective-permute-start.13
  131.7 4.7 %collective-permute-done.4 = bf16[1,256,1024]{2,1,0:T(8,128)(2,1)S(1)} collective-permute-done((bf16[1,256,1024]{2,1,0:T(8,128)(2,1)S(1)}, bf16[1,256,1024]{2,1,0:T(8,128)(2,1)S(1)}, u32[]{:S(2)}, u32[]{:S(2)}) %collective-permute-start.4) | collective-permute-done | bytes 524320 | tf_op jit(solution)/shard_map/ppermute | solution.py:199
  138.3 15.0 %collective-permute-done.17 = bf16[3,128,1024]{2,1,0:T(8,128)(2,1)S(1)} collective-permute-done((bf16[3,128,1024]{2,1,0:T(8,128)(2,1)S(1)}, bf16[3,128,1024]{2,1,0:T(8,128)(2,1)S(1)}, u32[]{:S(2)}, u32[]{:S(2)}) %collective-permute-start.17) | collective-permute-done | bytes 786464 | tf_op jit(solution)/shard_map/ppermute | solution.py:199
  154.1 16.0 %collective-permute-done.9 = bf16[3,128,1024]{2,1,0:T(8,128)(2,1)S(1)} collective-permute-done((bf16[3,128,1024]{2,1,0:T(8,128)(2,1)S(1)}, bf16[3,128,1024]{2,1,0:T(8,128)(2,1)S(1)}, u32[]{:S(2)}, u32[]{:S(2)}) %collective-permute-start.9) | collective-permute-done | bytes 786464 | tf_op jit(solution)/shard_map/ppermute | solution.py:199
  174.4 28.3 %collective-permute-done.10 = bf16[3,128,1024]{2,1,0:T(8,128)(2,1)S(1)} collective-permute-done((bf16[3,128,1024]{2,1,0:T(8,128)(2,1)S(1)}, bf16[3,128,1024]{2,1,0:T(8,128)(2,1)S(1)}, u32[]{:S(2)}, u32[]{:S(2)}) %collective-permute-start.10) | collective-permute-done | bytes 786464 | tf_op jit(solution)/shard_map/ppermute | solution.py:199
  206.7 2.4 collective-permute-done.6
  209.9 7.0 %input_grad_part.8.acc_in = f32[512,2048]{1,0:T(8,128)S(1)} custom-call(s32[25]{0:T(128)S(1)} %get-tuple-element.67.flags, bf16[3,256,1024]{2,1,0:T(8,128)(2,1)S(1)} %pad_maximum_fusion.3.delta.near, bf16[2048,4096]{1,0:T(8,128)(2,1)} %gate.15, bf16[2048,4096]{1,0:T(8,128)(2,1)} %up.15, ...), custom_call_target="tpu_custom_call", output_to_operand_aliasing={{}: (4, {})} | custom-call | flops 2147483648 | bytes 12582912 | tf_op jit(solution)/shard_map/input_grad_part/pallas_call | solution.py:102
  216.9 7.0 %input_grad_part.9.acc_in = f32[512,2048]{1,0:T(8,128)S(1)} custom-call(s32[25]{0:T(128)S(1)} %get-tuple-element.71.flags, bf16[3,256,1024]{2,1,0:T(8,128)(2,1)S(1)} %pad_maximum_fusion.2.delta.near, bf16[2048,4096]{1,0:T(8,128)(2,1)} %gate.15, bf16[2048,4096]{1,0:T(8,128)(2,1)} %up.15, ...), custom_call_target="tpu_custom_call", output_to_operand_aliasing={{}: (4, {})} | custom-call | flops 2147483648 | bytes 12582912 | tf_op jit(solution)/shard_map/input_grad_part/pallas_call | solution.py:102
  223.9 7.0 %input_grad_part.10.acc_in = f32[512,2048]{1,0:T(8,128)S(1)} custom-call(s32[25]{0:T(128)S(1)} %get-tuple-element.75.flags, bf16[3,256,1024]{2,1,0:T(8,128)(2,1)S(1)} %pad_maximum_fusion.1.delta.near, bf16[2048,4096]{1,0:T(8,128)(2,1)} %gate.15, bf16[2048,4096]{1,0:T(8,128)(2,1)} %up.15, ...), custom_call_target="tpu_custom_call", output_to_operand_aliasing={{}: (4, {})} | custom-call | flops 2147483648 | bytes 12582912 | tf_op jit(solution)/shard_map/input_grad_part/pallas_call | solution.py:102
  231.0 7.5 %input_grad_part.11.acc_in = f32[512,2048]{1,0:T(8,128)S(1)} custom-call(s32[25]{0:T(128)S(1)} %get-tuple-element.79.flags, bf16[3,256,1024]{2,1,0:T(8,128)(2,1)S(1)} %pad_maximum_fusion.delta.near, bf16[2048,4096]{1,0:T(8,128)(2,1)} %gate.15, bf16[2048,4096]{1,0:T(8,128)(2,1)} %up.15, ...), custom_call_target="tpu_custom_call", output_to_operand_aliasing={{}: (4, {})} | custom-call | flops 2147483648 | bytes 12582912 | tf_op jit(solution)/shard_map/input_grad_part/pallas_call | solution.py:102
  238.4 36.1 %collective-permute-done.19.delta.far = bf16[3,256,1024]{2,1,0:T(8,128)(2,1)S(1)} collective-permute-done((bf16[3,256,1024]{2,1,0:T(8,128)(2,1)S(1)}, bf16[3,256,1024]{2,1,0:T(8,128)(2,1)S(1)}, u32[]{:S(2)}, u32[]{:S(2)}) %collective-permute-start.19) | collective-permute-done | bytes 1572896 | tf_op jit(solution)/shard_map/ppermute | solution.py:199
  274.5 7.0 %input_grad_part.12.acc_in = f32[512,2048]{1,0:T(8,128)S(1)} custom-call(s32[25]{0:T(128)S(1)} %get-tuple-element.67.flags, bf16[3,256,1024]{2,1,0:T(8,128)(2,1)S(1)} %collective-permute-done.19.delta.far, bf16[2048,4096]{1,0:T(8,128)(2,1)} %gate.15, bf16[2048,4096]{1,0:T(8,128)(2,1)} %up.15, ...), custom_call_target="tpu_custom_call", output_to_operand_aliasing={{}: (4, {})} | custom-call | flops 2147483648 | bytes 12582912 | tf_op jit(solution)/shard_map/input_grad_part/pallas_call | solution.py:102
  281.5 7.0 %input_grad_part.13.acc_in = f32[512,2048]{1,0:T(8,128)S(1)} custom-call(s32[25]{0:T(128)S(1)} %get-tuple-element.71.flags, bf16[3,256,1024]{2,1,0:T(8,128)(2,1)S(1)} %collective-permute-done.15.delta.far, bf16[2048,4096]{1,0:T(8,128)(2,1)} %gate.15, bf16[2048,4096]{1,0:T(8,128)(2,1)} %up.15, ...), custom_call_target="tpu_custom_call", output_to_operand_aliasing={{}: (4, {})} | custom-call | flops 2147483648 | bytes 12582912 | tf_op jit(solution)/shard_map/input_grad_part/pallas_call | solution.py:102
  288.6 7.0 %input_grad_part.14.acc_in = f32[512,2048]{1,0:T(8,128)S(1)} custom-call(s32[25]{0:T(128)S(1)} %get-tuple-element.75.flags, bf16[3,256,1024]{2,1,0:T(8,128)(2,1)S(1)} %collective-permute-done.11.delta.far, bf16[2048,4096]{1,0:T(8,128)(2,1)} %gate.15, bf16[2048,4096]{1,0:T(8,128)(2,1)} %up.15, ...), custom_call_target="tpu_custom_call", output_to_operand_aliasing={{}: (4, {})} | custom-call | flops 2147483648 | bytes 12582912 | tf_op jit(solution)/shard_map/input_grad_part/pallas_call | solution.py:102
  295.6 7.5 %input_grad_part.15 = f32[512,2048]{1,0:T(8,128)S(1)} custom-call(s32[25]{0:T(128)S(1)} %get-tuple-element.79.flags, bf16[3,256,1024]{2,1,0:T(8,128)(2,1)S(1)} %collective-permute-done.7.delta.far, bf16[2048,4096]{1,0:T(8,128)(2,1)} %gate.15, bf16[2048,4096]{1,0:T(8,128)(2,1)} %up.15, ...), custom_call_target="tpu_custom_call", output_to_operand_aliasing={{}: (4, {})} | custom-call | flops 2147483648 | bytes 12582912 | tf_op jit(solution)/shard_map/input_grad_part/pallas_call | solution.py:102
  310.7 7.9 %weight_grad_part.4 = (bf16[2048,4096]{1,0:T(8,128)(2,1)}, bf16[2048,4096]{1,0:T(8,128)(2,1)}, bf16[4096,2048]{1,0:T(8,128)(2,1)}) custom-call(s32[25]{0:T(128)S(1)} %get-tuple-element.67.flags, bf16[3,256,1024]{2,1,0:T(8,128)(2,1)S(1)} %copy-done.12, bf16[3,256,1024]{2,1,0:T(8,128)(2,1)S(1)} %copy-done.28, bf16[512,2048]{1,0:T(8,128)(2,1)S(1)} %copy-done.2, ...), custom_call_target="tpu_custom_call" | custom-call | flops 6442450944 | bytes 16777216 | tf_op jit(solution)/shard_map/weight_grad_part/pallas_call | solution.py:155
  318.6 7.7 %weight_grad_part.5 = (bf16[2048,4096]{1,0:T(8,128)(2,1)}, bf16[2048,4096]{1,0:T(8,128)(2,1)}, bf16[4096,2048]{1,0:T(8,128)(2,1)}) custom-call(s32[25]{0:T(128)S(1)} %get-tuple-element.71.flags, bf16[3,256,1024]{2,1,0:T(8,128)(2,1)S(1)} %copy-done.10, ...), custom_call_target="tpu_custom_call", output_to_operand_aliasing={{0}: (5, {}), {1}: (6, {}), {2}: (7, {})} | custom-call | flops 6442450944 | bytes 16777216 | tf_op jit(solution)/shard_map/weight_grad_part/pallas_call | solution.py:155
  326.3 7.6 %weight_grad_part.6 = (bf16[2048,4096]{1,0:T(8,128)(2,1)}, bf16[2048,4096]{1,0:T(8,128)(2,1)}, bf16[4096,2048]{1,0:T(8,128)(2,1)}) custom-call(s32[25]{0:T(128)S(1)} %get-tuple-element.75.flags, bf16[3,256,1024]{2,1,0:T(8,128)(2,1)S(1)} %copy-done.6, ...), custom_call_target="tpu_custom_call", output_to_operand_aliasing={{0}: (5, {}), {1}: (6, {}), {2}: (7, {})} | custom-call | flops 6442450944 | bytes 16777216 | tf_op jit(solution)/shard_map/weight_grad_part/pallas_call | solution.py:155
  334.0 8.1 %weight_grad_part.7 = (bf16[2048,4096]{1,0:T(8,128)(2,1)}, bf16[2048,4096]{1,0:T(8,128)(2,1)}, bf16[4096,2048]{1,0:T(8,128)(2,1)}) custom-call(s32[25]{0:T(128)S(1)} %get-tuple-element.79.flags, bf16[3,256,1024]{2,1,0:T(8,128)(2,1)S(1)} %copy-done.8, ...), custom_call_target="tpu_custom_call", output_to_operand_aliasing={{0}: (5, {}), {1}: (6, {}), {2}: (7, {})} | custom-call | flops 6442450944 | bytes 16777216 | tf_op jit(solution)/shard_map/weight_grad_part/pallas_call | solution.py:155
  342.1 13.9 %reduce-scatter.2.cloned.1.call-done = f32[64,2048]{1,0:T(8,128)} async-done(((f32[512,2048]{1,0:T(8,128)}), f32[64,2048]{1,0:T(8,128)}) %reduce-scatter.2.cloned.1.call-update) | async-done | bytes 524304 | tf_op jit(solution)/shard_map/reduce_scatter | solution.py:280
  (144 shorter events, 45.7 us)
Async XLA Ops:
  7.2 34.3 %all-gather.3.cloned.1.call-start = ((), (), s32[]{:S(2)}) async-start(), calls=%async_computation.1 | async-start | bytes 2359296 | tf_op jit(solution)/shard_map/all_gather | solution.py:246
  7.9 79.1 %all-gather.5.cloned.1.call-start = ((), (), s32[]{:S(2)}) async-start(), calls=%async_computation.2 | async-start | bytes 2359296 | tf_op jit(solution)/shard_map/all_gather | solution.py:247
  8.6 347.4 %reduce-scatter.2.cloned.1.call-start = ((), (), s32[]{:S(2)}) async-start(), calls=%async_computation.3 | async-start | bytes 4718592 | tf_op jit(solution)/shard_map/reduce_scatter | solution.py:280
  52.8 42.3 %collective-permute-start = (bf16[2,256,1024]{2,1,0:T(8,128)(2,1)}, bf16[2,256,1024]{2,1,0:T(8,128)(2,1)}, u32[]{:S(2)}, u32[]{:S(2)}) collective-permute-start(bf16[2,256,1024]{2,1,0:T(8,128)(2,1)} %get-tuple-element.70), channel_id=1, source_target_pairs={{0,8},{8,0},{16,24},{24,16},{1,9},{9,1},{17,25},{25,17},{2,10},{10... | collective-permute-start | bytes 3145736 | tf_op jit(solution)/shard_map/ppermute | solution.py:199
  65.2 11.6 %copy-start.2 = (bf16[512,2048]{1,0:T(8,128)(2,1)S(1)}, bf16[512,2048]{1,0:T(8,128)(2,1)}, u32[]{:S(2)}) copy-start(bf16[512,2048]{1,0:T(8,128)(2,1)} %all-gather.3.cloned.1.call-done.acts.tokens) | copy-start | bytes 6291460
  65.2 36.9 %collective-permute-start.1 = (bf16[2,256,1024]{2,1,0:T(8,128)(2,1)}, bf16[2,256,1024]{2,1,0:T(8,128)(2,1)}, u32[]{:S(2)}, u32[]{:S(2)}) collective-permute-start(bf16[2,256,1024]{2,1,0:T(8,128)(2,1)} %get-tuple-element.74), channel_id=1, source_target_pairs={{0,16},{8,24},{16,0},{24,8},{1,17},{9,25},{17,1},{25,9},{2,18},{10... | collective-permute-start | bytes 3145736 | tf_op jit(solution)/shard_map/ppermute | solution.py:199
  74.3 37.0 %collective-permute-start.2 = (bf16[2,256,1024]{2,1,0:T(8,128)(2,1)S(1)}, bf16[2,256,1024]{2,1,0:T(8,128)(2,1)}, u32[]{:S(2)}, u32[]{:S(2)}) collective-permute-start(bf16[2,256,1024]{2,1,0:T(8,128)(2,1)S(1)} %get-tuple-element.78), channel_id=1, source_target_pairs={{0,8},{8,0},{16,24},{24,16},{1,9},{9,1},{17,25},{25,17},{2,10},{10... | collective-permute-start | bytes 3145736 | tf_op jit(solution)/shard_map/ppermute | solution.py:199
  87.0 34.0 %collective-permute-start.3 = (bf16[2,256,1024]{2,1,0:T(8,128)(2,1)}, bf16[2,256,1024]{2,1,0:T(8,128)(2,1)}, u32[]{:S(2)}, u32[]{:S(2)}) collective-permute-start(bf16[2,256,1024]{2,1,0:T(8,128)(2,1)} %get-tuple-element.82), channel_id=1, source_target_pairs={{0,16},{8,24},{16,0},{24,8},{1,17},{9,25},{17,1},{25,9},{2,18},{10... | collective-permute-start | bytes 3145736 | tf_op jit(solution)/shard_map/ppermute | solution.py:199
  95.1 29.8 %collective-permute-start.16 = (bf16[1,256,1024]{2,1,0:T(8,128)(2,1)S(1)}, bf16[1,256,1024]{2,1,0:T(8,128)(2,1)}, u32[]{:S(2)}, u32[]{:S(2)}) collective-permute-start(bf16[1,256,1024]{2,1,0:T(8,128)(2,1)S(1)} %get-tuple-element.101), channel_id=1, source_target_pairs={{0,8},{8,0},{16,24},{24,16},{1,9},{9,1},{17,25},{25,17},{2,10},{10... | collective-permute-start | bytes 1572872 | tf_op jit(solution)/shard_map/ppermute | solution.py:199
  102.1 9.3 %copy-start.22 = (f32[2,256,1024]{2,1,0:T(8,128)S(1)}, f32[2,256,1024]{2,1,0:T(8,128)}, u32[]{:S(2)}) copy-start(f32[2,256,1024]{2,1,0:T(8,128)} %copy-done.21) | copy-start | bytes 6291460
  102.1 25.7 %collective-permute-start.12 = (bf16[1,256,1024]{2,1,0:T(8,128)(2,1)S(1)}, bf16[1,256,1024]{2,1,0:T(8,128)(2,1)}, u32[]{:S(2)}, u32[]{:S(2)}) collective-permute-start(bf16[1,256,1024]{2,1,0:T(8,128)(2,1)S(1)} %get-tuple-element.95), channel_id=1, source_target_pairs={{0,16},{8,24},{16,0},{24,8},{1,17},{9,25},{17,1},{25,9},{2,18},{10... | collective-permute-start | bytes 1572872 | tf_op jit(solution)/shard_map/ppermute | solution.py:199
  111.3 19.8 %collective-permute-start.8 = (bf16[1,256,1024]{2,1,0:T(8,128)(2,1)S(1)}, bf16[1,256,1024]{2,1,0:T(8,128)(2,1)S(1)}, u32[]{:S(2)}, u32[]{:S(2)}) collective-permute-start(bf16[1,256,1024]{2,1,0:T(8,128)(2,1)S(1)} %get-tuple-element.89), channel_id=1, source_target_pairs={{0,8},{8,0},{16,24},{24,16},{1,9},{9,1},{17,25},{25,17},{2,10},{10... | collective-permute-start | bytes 1572872 | tf_op jit(solution)/shard_map/ppermute | solution.py:199
  121.1 15.3 %collective-permute-start.4 = (bf16[1,256,1024]{2,1,0:T(8,128)(2,1)S(1)}, bf16[1,256,1024]{2,1,0:T(8,128)(2,1)S(1)}, u32[]{:S(2)}, u32[]{:S(2)}) collective-permute-start(bf16[1,256,1024]{2,1,0:T(8,128)(2,1)S(1)} %get-tuple-element.83), channel_id=1, source_target_pairs={{0,16},{8,24},{16,0},{24,8},{1,17},{9,25},{17,1},{25,9},{2,18},{10... | collective-permute-start | bytes 1572872 | tf_op jit(solution)/shard_map/ppermute | solution.py:199
  126.3 27.0 %collective-permute-start.17 = (bf16[3,128,1024]{2,1,0:T(8,128)(2,1)S(1)}, bf16[3,128,1024]{2,1,0:T(8,128)(2,1)S(1)}, u32[]{:S(2)}, u32[]{:S(2)}) collective-permute-start(bf16[3,128,1024]{2,1,0:T(8,128)(2,1)S(1)} %pad_maximum_fusion.10), channel_id=1, source_target_pairs={{0,16},{8,24},{16,0},{24,8},{1,17},{9,25},{17,1},{25,9},{2,18},{10... | collective-permute-start | bytes 2359304 | tf_op jit(solution)/shard_map/ppermute | solution.py:199
  129.1 41.9 %collective-permute-start.13 = (bf16[3,128,1024]{2,1,0:T(8,128)(2,1)S(1)}, bf16[3,128,1024]{2,1,0:T(8,128)(2,1)S(1)}, u32[]{:S(2)}, u32[]{:S(2)}) collective-permute-start(bf16[3,128,1024]{2,1,0:T(8,128)(2,1)S(1)} %pad_maximum_fusion.8), channel_id=1, source_target_pairs={{0,8},{8,0},{16,24},{24,16},{1,9},{9,1},{17,25},{25,17},{2,10},{10... | collective-permute-start | bytes 2359304 | tf_op jit(solution)/shard_map/ppermute | solution.py:199
  131.5 38.7 %collective-permute-start.9 = (bf16[3,128,1024]{2,1,0:T(8,128)(2,1)S(1)}, bf16[3,128,1024]{2,1,0:T(8,128)(2,1)S(1)}, u32[]{:S(2)}, u32[]{:S(2)}) collective-permute-start(bf16[3,128,1024]{2,1,0:T(8,128)(2,1)S(1)} %pad_maximum_fusion.6), channel_id=1, source_target_pairs={{0,16},{8,24},{16,0},{24,8},{1,17},{9,25},{17,1},{25,9},{2,18},{10... | collective-permute-start | bytes 2359304 | tf_op jit(solution)/shard_map/ppermute | solution.py:199
  136.7 36.4 %collective-permute-start.5 = (bf16[3,128,1024]{2,1,0:T(8,128)(2,1)S(1)}, bf16[3,128,1024]{2,1,0:T(8,128)(2,1)S(1)}, u32[]{:S(2)}, u32[]{:S(2)}) collective-permute-start(bf16[3,128,1024]{2,1,0:T(8,128)(2,1)S(1)} %pad_maximum_fusion.4), channel_id=1, source_target_pairs={{0,8},{8,0},{16,24},{24,16},{1,9},{9,1},{17,25},{25,17},{2,10},{10... | collective-permute-start | bytes 2359304 | tf_op jit(solution)/shard_map/ppermute | solution.py:199
  153.9 49.5 %collective-permute-start.18 = (bf16[3,128,1024]{2,1,0:T(8,128)(2,1)S(1)}, bf16[3,128,1024]{2,1,0:T(8,128)(2,1)S(1)}, u32[]{:S(2)}, u32[]{:S(2)}) collective-permute-start(bf16[3,128,1024]{2,1,0:T(8,128)(2,1)S(1)} %pad_maximum_fusion.11), channel_id=1, source_target_pairs={{0,16},{8,24},{16,0},{24,8},{1,17},{9,25},{17,1},{25,9},{2,18},{10... | collective-permute-start | bytes 2359304 | tf_op jit(solution)/shard_map/ppermute | solution.py:199
  170.8 32.0 %collective-permute-start.10 = (bf16[3,128,1024]{2,1,0:T(8,128)(2,1)S(1)}, bf16[3,128,1024]{2,1,0:T(8,128)(2,1)S(1)}, u32[]{:S(2)}, u32[]{:S(2)}) collective-permute-start(bf16[3,128,1024]{2,1,0:T(8,128)(2,1)S(1)} %pad_maximum_fusion.7), channel_id=1, source_target_pairs={{0,16},{8,24},{16,0},{24,8},{1,17},{9,25},{17,1},{25,9},{2,18},{10... | collective-permute-start | bytes 2359304 | tf_op jit(solution)/shard_map/ppermute | solution.py:199
  171.7 33.8 %collective-permute-start.14 = (bf16[3,128,1024]{2,1,0:T(8,128)(2,1)S(1)}, bf16[3,128,1024]{2,1,0:T(8,128)(2,1)S(1)}, u32[]{:S(2)}, u32[]{:S(2)}) collective-permute-start(bf16[3,128,1024]{2,1,0:T(8,128)(2,1)S(1)} %pad_maximum_fusion.9), channel_id=1, source_target_pairs={{0,8},{8,0},{16,24},{24,16},{1,9},{9,1},{17,25},{25,17},{2,10},{10... | collective-permute-start | bytes 2359304 | tf_op jit(solution)/shard_map/ppermute | solution.py:199
  173.7 35.4 %collective-permute-start.6 = (bf16[3,128,1024]{2,1,0:T(8,128)(2,1)S(1)}, bf16[3,128,1024]{2,1,0:T(8,128)(2,1)S(1)}, u32[]{:S(2)}, u32[]{:S(2)}) collective-permute-start(bf16[3,128,1024]{2,1,0:T(8,128)(2,1)S(1)} %pad_maximum_fusion.5), channel_id=1, source_target_pairs={{0,8},{8,0},{16,24},{24,16},{1,9},{9,1},{17,25},{25,17},{2,10},{10... | collective-permute-start | bytes 2359304 | tf_op jit(solution)/shard_map/ppermute | solution.py:199
  203.0 20.9 %copy-start.5 = (bf16[3,256,1024]{2,1,0:T(8,128)(2,1)}, bf16[3,256,1024]{2,1,0:T(8,128)(2,1)S(1)}, u32[]{:S(2)}) copy-start(bf16[3,256,1024]{2,1,0:T(8,128)(2,1)S(1)} %pad_maximum_fusion.1.delta.near) | copy-start | bytes 4718596
  203.0 85.5 %collective-permute-start.11 = (bf16[3,256,1024]{2,1,0:T(8,128)(2,1)S(1)}, bf16[3,256,1024]{2,1,0:T(8,128)(2,1)S(1)}, u32[]{:S(2)}, u32[]{:S(2)}) collective-permute-start(bf16[3,256,1024]{2,1,0:T(8,128)(2,1)S(1)} %pad_maximum_fusion.1.delta.near), channel_id=1, source_target_pairs={{0,8},{8,0},{16,24},{24,16},{1,9},{9,1},{17,25},{25,17},{2,10},{10... | collective-permute-start | bytes 4718600 | tf_op jit(solution)/shard_map/ppermute | solution.py:199
  203.7 70.9 %collective-permute-start.19 = (bf16[3,256,1024]{2,1,0:T(8,128)(2,1)S(1)}, bf16[3,256,1024]{2,1,0:T(8,128)(2,1)S(1)}, u32[]{:S(2)}, u32[]{:S(2)}) collective-permute-start(bf16[3,256,1024]{2,1,0:T(8,128)(2,1)S(1)} %pad_maximum_fusion.3.delta.near), channel_id=1, source_target_pairs={{0,8},{8,0},{16,24},{24,16},{1,9},{9,1},{17,25},{25,17},{2,10},{10... | collective-permute-start | bytes 4718600 | tf_op jit(solution)/shard_map/ppermute | solution.py:199
  205.7 11.2 %copy-start.9 = (bf16[3,256,1024]{2,1,0:T(8,128)(2,1)}, bf16[3,256,1024]{2,1,0:T(8,128)(2,1)S(1)}, u32[]{:S(2)}) copy-start(bf16[3,256,1024]{2,1,0:T(8,128)(2,1)S(1)} %pad_maximum_fusion.2.delta.near) | copy-start | bytes 4718596
  205.7 75.8 %collective-permute-start.15 = (bf16[3,256,1024]{2,1,0:T(8,128)(2,1)S(1)}, bf16[3,256,1024]{2,1,0:T(8,128)(2,1)S(1)}, u32[]{:S(2)}, u32[]{:S(2)}) collective-permute-start(bf16[3,256,1024]{2,1,0:T(8,128)(2,1)S(1)} %pad_maximum_fusion.2.delta.near), channel_id=1, source_target_pairs={{0,16},{8,24},{16,0},{24,8},{1,17},{9,25},{17,1},{25,9},{2,18},{10... | collective-permute-start | bytes 4718600 | tf_op jit(solution)/shard_map/ppermute | solution.py:199
  209.3 21.6 %copy-start.7 = (bf16[3,256,1024]{2,1,0:T(8,128)(2,1)}, bf16[3,256,1024]{2,1,0:T(8,128)(2,1)S(1)}, u32[]{:S(2)}) copy-start(bf16[3,256,1024]{2,1,0:T(8,128)(2,1)S(1)} %pad_maximum_fusion.delta.near) | copy-start | bytes 4718596
  209.3 86.3 %collective-permute-start.7 = (bf16[3,256,1024]{2,1,0:T(8,128)(2,1)S(1)}, bf16[3,256,1024]{2,1,0:T(8,128)(2,1)S(1)}, u32[]{:S(2)}, u32[]{:S(2)}) collective-permute-start(bf16[3,256,1024]{2,1,0:T(8,128)(2,1)S(1)} %pad_maximum_fusion.delta.near), channel_id=1, source_target_pairs={{0,16},{8,24},{16,0},{24,8},{1,17},{9,25},{17,1},{25,9},{2,18},{10... | collective-permute-start | bytes 4718600 | tf_op jit(solution)/shard_map/ppermute | solution.py:199
  310.7 7.9 %copy-start.10 = (bf16[3,256,1024]{2,1,0:T(8,128)(2,1)S(1)}, bf16[3,256,1024]{2,1,0:T(8,128)(2,1)}, u32[]{:S(2)}) copy-start(bf16[3,256,1024]{2,1,0:T(8,128)(2,1)} %copy-done.9) | copy-start | bytes 4718596
  310.7 7.9 %copy-start.18 = (bf16[3,256,1024]{2,1,0:T(8,128)(2,1)S(1)}, bf16[3,256,1024]{2,1,0:T(8,128)(2,1)}, u32[]{:S(2)}) copy-start(bf16[3,256,1024]{2,1,0:T(8,128)(2,1)} %copy-done.17) | copy-start | bytes 4718596
  318.6 7.7 %copy-start.6 = (bf16[3,256,1024]{2,1,0:T(8,128)(2,1)S(1)}, bf16[3,256,1024]{2,1,0:T(8,128)(2,1)}, u32[]{:S(2)}) copy-start(bf16[3,256,1024]{2,1,0:T(8,128)(2,1)} %copy-done.5) | copy-start | bytes 4718596
  318.6 7.7 %copy-start.14 = (bf16[3,256,1024]{2,1,0:T(8,128)(2,1)S(1)}, bf16[3,256,1024]{2,1,0:T(8,128)(2,1)}, u32[]{:S(2)}) copy-start(bf16[3,256,1024]{2,1,0:T(8,128)(2,1)} %copy-done.13) | copy-start | bytes 4718596
  (20 other events, 69.5 us)
Sparse Core Ops, SparseCore 0:
  9.6 31.7 all-gather.2
  43.0 28.5 all-gather.4
  306.4 49.5 reduce-scatter.1
